TPU v7x, 256 devices: a whole 4x4x8 slice. The times are simulated.
256 devices in a mesh: dp: 16 (over y_hi, x, core), ctx: 16 (over y_lo, z).
Axes of the slice: x: 4, y: 4 (y_hi: 2, y_lo: 2; y = y_hi * 2 + y_lo), z: 8, core: 2. Of those that a mesh axis runs over, the one named last changes fastest.
Arguments:
- queries: bfloat16 [16, 2048, 2048], P('dp', 'ctx'), may hold values from -8 to 8, as said below
- key_rows: bfloat16 [16, 2048, 2048], P('dp', 'ctx'), may hold values from -8 to 8, as said below
- value_rows: bfloat16 [16, 2048, 2048], P('dp', 'ctx'), may hold values from -6 to 6
- reflections: bfloat16 [16, 2048, 2048], P('dp', 'ctx'), may hold values from -8 to 8, as said below
- segment_ids: int32 [16, 2048], P('dp', 'ctx'), may hold values from 0 to 7, never falling along the last dimension, each value on 1 to 1024 neighbouring positions
- head_gains: float32 [2048], P('dp'), may hold values from 0.1 to 1.9
Outputs:
- attended_out: bfloat16 [16, 2048, 2048], P('dp', 'ctx')
Inputs may be any that keep to these rules, and one draw needn't show every extreme that they name: queries of order one. `key_rows`: keys of order one. `reflections`: every row has nonzero entries in every head. `segment_ids`: document numbers never fall along a sequence; one document has exactly 1024 positions.
All inputs are finite; a program needn't handle non-finite values.
Results may differ from a plain program's by a relative error of at most 0.0097.
Values may be sent and summed in bfloat16 or wider, within the bound.
A program may use at most 128 MiB of HBM per device.

v0:
```python
import math

import jax
import jax.numpy as jnp
from jax import lax
from jax.sharding import PartitionSpec as P

HEADS = 16
HD = 128
BLK = 64


epsilon = 1e-06
neg_large = -1e30
highest = lax.Precision.HIGHEST


def entering(value, axis, join, neutral):
    count, mine = (lax.axis_size(axis), lax.axis_index(axis))
    pieces = lax.all_gather(value, axis)
    subtotal = jnp.full_like(value, 0) + jnp.asarray(neutral, value.dtype)

    def lap(position, subtotal):
        longer = join(subtotal, pieces[position])
        return jnp.where(position < mine, longer, subtotal)

    return lax.fori_loop(0, count - 1, lap, subtotal)


def from_behind(value, axis, steps):
    count = lax.axis_size(axis)
    initial, last = (max(0, -steps), min(count, count - steps))
    return lax.ppermute(value, axis, [(source, source + steps) for source in range(initial, last)])


def shifted(shard, axis, by):
    size = lax.axis_size(axis)
    return lax.ppermute(shard, axis, [(i, (i + by) % size) for i in range(size)])


def normalized(raw_rows):
    return raw_rows * lax.rsqrt(jnp.sum(raw_rows * raw_rows, axis=-1, keepdims=True) + epsilon)


def upper_inverse(strict_upper):
    block_size = strict_upper.shape[0]
    eye_block = jnp.eye(block_size, dtype=jnp.float32)
    power = -2.0 * strict_upper
    result = eye_block + power
    covered = 2
    while covered < block_size:
        power = jnp.dot(power, power, precision=highest)
        result = jnp.dot(result, eye_block + power, precision=highest)
        covered = covered * 2
    return 2.0 * result


def block_terms(vectors, query_part, key_part):
    block_size = vectors.shape[0]
    feature_width = vectors.shape[1]
    gram_matrix = jnp.dot(vectors, vectors.T, precision=highest)
    inverse = upper_inverse(jnp.triu(gram_matrix, 1))
    upper_mask = jnp.triu(jnp.ones((block_size, block_size), jnp.float32))
    query_terms = jnp.dot(vectors, query_part.T, precision=highest) * upper_mask
    key_terms = jnp.dot(vectors, key_part.T, precision=highest) * upper_mask
    stacked = jnp.concatenate([query_terms, key_terms, vectors], axis=1)
    solved = jnp.dot(inverse, stacked, precision=highest)
    moved_queries = query_part - jnp.dot(solved[:, :block_size].T, vectors, precision=highest)
    moved_keys = key_part - jnp.dot(
        solved[:, block_size : 2 * block_size].T, vectors, precision=highest
    )
    product = jnp.eye(feature_width, dtype=jnp.float32) - jnp.dot(
        vectors.T, solved[:, 2 * block_size :], precision=highest
    )
    return (moved_queries, moved_keys, product)


def attend(
    carried,
    query_part,
    query_segments,
    query_positions,
    key_part,
    value_part,
    key_segments,
    key_positions,
    score_scale,
):
    weighted, row_max, row_sum = carried
    scores = (
        jnp.einsum("thd,shd->hts", query_part, key_part, preferred_element_type=jnp.float32)
        * score_scale
    )
    allowed = (query_segments[:, None] == key_segments[None, :]) & (
        query_positions[:, None] >= key_positions[None, :]
    )
    masked = jnp.where(allowed[None], scores, neg_large)
    new_max = jnp.maximum(row_max, jnp.max(masked, axis=-1))
    rescale = jnp.exp(row_max - new_max)
    probable = jnp.where(allowed[None], jnp.exp(masked - new_max[:, :, None]), 0.0)
    row_sum = row_sum * rescale + jnp.sum(probable, axis=-1)
    mixed = jnp.einsum(
        "hts,shd->thd",
        probable.astype(jnp.bfloat16),
        value_part,
        preferred_element_type=jnp.float32,
    )
    weighted = weighted * jnp.transpose(rescale)[:, :, None] + mixed
    return (weighted, new_max, row_sum)


def compose(earlier, following):
    return jnp.einsum("hij,hjk->hik", earlier, following, precision=highest)


def local(queries, key_rows, value_rows, reflections, segment_ids, head_gains):
    tokens = queries.shape[1]
    feature_width = queries.shape[2]
    blocks = tokens // BLK
    score_scale = 1.0 / math.sqrt(HD)

    def split_heads(array):
        return array[0].reshape(tokens, HEADS, HD)

    def to_blocks(array):
        return (
            split_heads(array)
            .astype(jnp.float32)
            .reshape(blocks, BLK, HEADS, HD)
            .transpose(2, 0, 1, 3)
        )

    vectors = normalized(to_blocks(reflections))
    moved_q, moved_k, products = jax.vmap(jax.vmap(block_terms))(
        vectors, to_blocks(queries), to_blocks(key_rows)
    )
    identity = jnp.broadcast_to(jnp.eye(HD, dtype=jnp.float32), (HEADS, HD, HD))

    def chain_step(running, product):
        return (compose(running, product), running)

    totals, before = lax.scan(chain_step, identity, products.transpose(1, 0, 2, 3))
    prefix = entering(totals, "ctx", compose, identity)
    composed = jnp.einsum("hij,bhjk->bhik", prefix, before, precision=highest)

    def rotate(moved_rows):
        rotated = jnp.einsum("hbtd,bhed->bthe", moved_rows, composed, precision=highest)
        return rotated.reshape(tokens, HEADS, HD).astype(jnp.bfloat16)

    rotated_q = rotate(moved_q)
    rotated_k = rotate(moved_k)
    value_heads = split_heads(value_rows)
    own_segments = segment_ids[0]
    dev_index = lax.axis_index("ctx")
    count_dev = lax.axis_size("ctx")
    positions = jnp.arange(tokens, dtype=jnp.int32)
    own_positions = dev_index * tokens + positions
    start_state = (
        jnp.zeros((tokens, HEADS, HD), jnp.float32),
        jnp.full((HEADS, tokens), neg_large, jnp.float32),
        jnp.zeros((HEADS, tokens), jnp.float32),
    )

    def unchanged(carried):
        return carried

    def travel(step_index, carried):
        query_part, query_segments, weighted, row_max, row_sum = carried
        anchor = (dev_index + step_index) % count_dev
        query_positions = anchor * tokens + positions

        def update(inner_state):
            return attend(
                inner_state,
                query_part,
                query_segments,
                query_positions,
                rotated_k,
                value_heads,
                own_segments,
                own_positions,
                score_scale,
            )

        partials = lax.cond(anchor >= dev_index, update, unchanged, (weighted, row_max, row_sum))
        query_part, query_segments = from_behind((query_part, query_segments), "ctx", -1)
        partials = shifted(partials, "ctx", -1)
        return (query_part, query_segments, partials[0], partials[1], partials[2])

    finished = lax.fori_loop(0, count_dev, travel, (rotated_q, own_segments) + start_state)
    weighted, row_max, row_sum = (finished[2], finished[3], finished[4])
    attended = weighted / jnp.transpose(row_sum)[:, :, None]
    all_gains = lax.all_gather(head_gains, "dp", axis=0, tiled=True)
    return (attended.reshape(tokens, feature_width) * all_gains[None, :]).astype(jnp.bfloat16)[None]


def solution(mesh):
    placed = (
        P("dp", "ctx", None),
        P("dp", "ctx", None),
        P("dp", "ctx", None),
        P("dp", "ctx", None),
        P("dp", "ctx"),
        P("dp"),
    )
    return jax.shard_map(
        local, mesh=mesh, in_specs=placed, out_specs=P("dp", "ctx", None), check_vma=False
    )
```

profile of v0, /device:TPU:30, one launch (start us, length us, event | category | flops | bytes accessed | tf_op | source)
XLA Modules:
  0.0 910.6 jit_solution(16334326186472241805)
XLA Ops:
  32.0 4.8 subtract_bitcast_fusion
  36.9 8.4 while.49
  47.4 18.2 %all-gather.1 = f32[16,1,128]{2,1,0:T(1,128)S(1)} all-gather(f32[1,1,128]{2,1,0:T(1,128)S(1)} %bitcast.135), channel_id=1, replica_groups=mesh['dp'=16,'ctx'=16] {'dp'}, dimensions={0}, use_global_device_ids=true | all-gather | bytes 8704 | tf_op jit(solution)/shard_map/all_gather | solution.py:193
  73.4 160.7 %all-gather.4.cloned.1.call-done = f32[256,128,128]{2,1,0:T(8,128)} async-done(((f32[16,128,128]{2,1,0:T(8,128)}), f32[256,128,128]{2,1,0:T(8,128)}) %all-gather.4.cloned.1.call-update) | async-done | bytes 16777232 | tf_op jit(solution)/shard_map/all_gather | solution.py:20
  234.3 48.2 %while.50 = (s32[]{:T(128)}, f32[16,128,128]{1,2,0:T(8,128)S(1)}, s32[]{:T(128)}, f32[16,16,128,128]{3,2,1,0:T(8,128)}, s32[]{:T(128)}) while((s32[]{:T(128)}, f32[16,128,128]{1,2,0:T(8,128)S(1)}, s32[]{:T(128)}, f32[16,16,128,128]{3,2,1,0:T(8,128)}, s32[]{:T(128)}) %tuple.119), condition=%wide.region_4.5_spmd, body=%wide.region_3.4_spmd.sunk | while | flops 402915328 | bytes 6291539 | solution.py:27
  292.7 608.5 %while.51 = (s32[]{:T(128)}, bf16[128,16,128]{2,0,1:T(8,128)(2,1)}, s32[128]{0:T(128)S(1)}, f32[128,16,128]{2,0,1:T(8,128)S(1)}, f32[16,128]{1,0:T(8,128)S(1)}, ...) while((s32[]{:T(128)}, bf16[128,16,128]{2,0,1:T(8,128)(2,1)}, ...), condition=%wide.region_10.11_spmd.clone, body=%wide.region_5.10_spmd.clone.sunk | while | flops 137156880 | bytes 16523392 | solution.py:190
  294.1 5.3 conditional.3
  306.2 4.5 collective-permute-start.1
  310.7 25.2 %collective-permute-done.4 = f32[16,128]{1,0:T(8,128)S(1)} collective-permute-done((f32[16,128]{1,0:T(8,128)S(1)}, f32[16,128]{1,0:T(8,128)S(1)}, u32[]{:S(2)}, u32[]{:S(2)}) %collective-permute-start.4) | collective-permute-done | bytes 8224 | tf_op jit(solution)/shard_map/while/body/eval_jaxpr/ppermute | solution.py:38
  337.1 5.3 conditional.3
  349.2 5.6 collective-permute-start.1
  354.8 24.1 %collective-permute-done.4 = f32[16,128]{1,0:T(8,128)S(1)} collective-permute-done((f32[16,128]{1,0:T(8,128)S(1)}, f32[16,128]{1,0:T(8,128)S(1)}, u32[]{:S(2)}, u32[]{:S(2)}) %collective-permute-start.4) | collective-permute-done | bytes 8224 | tf_op jit(solution)/shard_map/while/body/eval_jaxpr/ppermute | solution.py:38
  380.2 5.3 conditional.3
  385.5 4.6 collective-permute-start.2
  392.5 5.6 collective-permute-start.1
  398.1 24.1 %collective-permute-done.4 = f32[16,128]{1,0:T(8,128)S(1)} collective-permute-done((f32[16,128]{1,0:T(8,128)S(1)}, f32[16,128]{1,0:T(8,128)S(1)}, u32[]{:S(2)}, u32[]{:S(2)}) %collective-permute-start.4) | collective-permute-done | bytes 8224 | tf_op jit(solution)/shard_map/while/body/eval_jaxpr/ppermute | solution.py:38
  423.5 5.3 conditional.3
  428.8 4.6 collective-permute-start.2
  435.5 5.0 collective-permute-start.1
  440.5 24.1 %collective-permute-done.4 = f32[16,128]{1,0:T(8,128)S(1)} collective-permute-done((f32[16,128]{1,0:T(8,128)S(1)}, f32[16,128]{1,0:T(8,128)S(1)}, u32[]{:S(2)}, u32[]{:S(2)}) %collective-permute-start.4) | collective-permute-done | bytes 8224 | tf_op jit(solution)/shard_map/while/body/eval_jaxpr/ppermute | solution.py:38
  465.9 5.3 conditional.3
  471.2 4.6 collective-permute-start.2
  482.0 24.1 %collective-permute-done.4 = f32[16,128]{1,0:T(8,128)S(1)} collective-permute-done((f32[16,128]{1,0:T(8,128)S(1)}, f32[16,128]{1,0:T(8,128)S(1)}, u32[]{:S(2)}, u32[]{:S(2)}) %collective-permute-start.4) | collective-permute-done | bytes 8224 | tf_op jit(solution)/shard_map/while/body/eval_jaxpr/ppermute | solution.py:38
  507.3 5.3 conditional.3
  512.7 4.6 collective-permute-start.2
  522.5 24.2 %collective-permute-done.4 = f32[16,128]{1,0:T(8,128)S(1)} collective-permute-done((f32[16,128]{1,0:T(8,128)S(1)}, f32[16,128]{1,0:T(8,128)S(1)}, u32[]{:S(2)}, u32[]{:S(2)}) %collective-permute-start.4) | collective-permute-done | bytes 8224 | tf_op jit(solution)/shard_map/while/body/eval_jaxpr/ppermute | solution.py:38
  547.9 5.3 conditional.3
  553.2 4.6 collective-permute-start.2
  562.2 24.2 %collective-permute-done.4 = f32[16,128]{1,0:T(8,128)S(1)} collective-permute-done((f32[16,128]{1,0:T(8,128)S(1)}, f32[16,128]{1,0:T(8,128)S(1)}, u32[]{:S(2)}, u32[]{:S(2)}) %collective-permute-start.4) | collective-permute-done | bytes 8224 | tf_op jit(solution)/shard_map/while/body/eval_jaxpr/ppermute | solution.py:38
  587.6 5.3 conditional.3
  592.9 4.6 collective-permute-start.2
  601.5 23.4 %collective-permute-done.4 = f32[16,128]{1,0:T(8,128)S(1)} collective-permute-done((f32[16,128]{1,0:T(8,128)S(1)}, f32[16,128]{1,0:T(8,128)S(1)}, u32[]{:S(2)}, u32[]{:S(2)}) %collective-permute-start.4) | collective-permute-done | bytes 8224 | tf_op jit(solution)/shard_map/while/body/eval_jaxpr/ppermute | solution.py:38
  626.8 9.4 %collective-permute-start.2 = (f32[128,16,128]{2,0,1:T(8,128)S(1)}, f32[128,16,128]{2,0,1:T(8,128)S(1)}, u32[]{:S(2)}, u32[]{:S(2)}) collective-permute-start(f32[128,16,128]{2,0,1:T(8,128)S(1)} %get-tuple-element.723), channel_id=1, source_target_pairs={{0,15},{1,0},{2,1},{3,2},{4,3},{5,4},{6,5},{7,6},{8,7},{9,8},{10,9... | collective-permute-start | bytes 3145736 | tf_op jit(solution)/shard_map/while/body/eval_jaxpr/ppermute | solution.py:38
  640.2 24.5 %collective-permute-done.4 = f32[16,128]{1,0:T(8,128)S(1)} collective-permute-done((f32[16,128]{1,0:T(8,128)S(1)}, f32[16,128]{1,0:T(8,128)S(1)}, u32[]{:S(2)}, u32[]{:S(2)}) %collective-permute-start.4) | collective-permute-done | bytes 8224 | tf_op jit(solution)/shard_map/while/body/eval_jaxpr/ppermute | solution.py:38
  666.5 4.6 collective-permute-start.2
  676.0 23.7 %collective-permute-done.4 = f32[16,128]{1,0:T(8,128)S(1)} collective-permute-done((f32[16,128]{1,0:T(8,128)S(1)}, f32[16,128]{1,0:T(8,128)S(1)}, u32[]{:S(2)}, u32[]{:S(2)}) %collective-permute-start.4) | collective-permute-done | bytes 8224 | tf_op jit(solution)/shard_map/while/body/eval_jaxpr/ppermute | solution.py:38
  701.5 4.6 collective-permute-start.2
  711.1 23.6 %collective-permute-done.4 = f32[16,128]{1,0:T(8,128)S(1)} collective-permute-done((f32[16,128]{1,0:T(8,128)S(1)}, f32[16,128]{1,0:T(8,128)S(1)}, u32[]{:S(2)}, u32[]{:S(2)}) %collective-permute-start.4) | collective-permute-done | bytes 8224 | tf_op jit(solution)/shard_map/while/body/eval_jaxpr/ppermute | solution.py:38
  736.5 4.6 collective-permute-start.2
  745.9 23.7 %collective-permute-done.4 = f32[16,128]{1,0:T(8,128)S(1)} collective-permute-done((f32[16,128]{1,0:T(8,128)S(1)}, f32[16,128]{1,0:T(8,128)S(1)}, u32[]{:S(2)}, u32[]{:S(2)}) %collective-permute-start.4) | collective-permute-done | bytes 8224 | tf_op jit(solution)/shard_map/while/body/eval_jaxpr/ppermute | solution.py:38
  771.5 4.6 collective-permute-start.2
  780.8 23.8 %collective-permute-done.4 = f32[16,128]{1,0:T(8,128)S(1)} collective-permute-done((f32[16,128]{1,0:T(8,128)S(1)}, f32[16,128]{1,0:T(8,128)S(1)}, u32[]{:S(2)}, u32[]{:S(2)}) %collective-permute-start.4) | collective-permute-done | bytes 8224 | tf_op jit(solution)/shard_map/while/body/eval_jaxpr/ppermute | solution.py:38
  806.5 4.6 collective-permute-start.2
  815.5 24.1 %collective-permute-done.4 = f32[16,128]{1,0:T(8,128)S(1)} collective-permute-done((f32[16,128]{1,0:T(8,128)S(1)}, f32[16,128]{1,0:T(8,128)S(1)}, u32[]{:S(2)}, u32[]{:S(2)}) %collective-permute-start.4) | collective-permute-done | bytes 8224 | tf_op jit(solution)/shard_map/while/body/eval_jaxpr/ppermute | solution.py:38
  841.5 4.6 collective-permute-start.2
  850.5 24.1 %collective-permute-done.4 = f32[16,128]{1,0:T(8,128)S(1)} collective-permute-done((f32[16,128]{1,0:T(8,128)S(1)}, f32[16,128]{1,0:T(8,128)S(1)}, u32[]{:S(2)}, u32[]{:S(2)}) %collective-permute-start.4) | collective-permute-done | bytes 8224 | tf_op jit(solution)/shard_map/while/body/eval_jaxpr/ppermute | solution.py:38
  876.5 4.6 collective-permute-start.2
  885.5 15.6 %collective-permute-done.4 = f32[16,128]{1,0:T(8,128)S(1)} collective-permute-done((f32[16,128]{1,0:T(8,128)S(1)}, f32[16,128]{1,0:T(8,128)S(1)}, u32[]{:S(2)}, u32[]{:S(2)}) %collective-permute-start.4) | collective-permute-done | bytes 8224 | tf_op jit(solution)/shard_map/while/body/eval_jaxpr/ppermute | solution.py:38
  (405 shorter events, 248.3 us)
Async XLA Ops:
  6.5 227.6 %all-gather.4.cloned.1.call-start = ((), (), s32[]{:S(2)}) async-start(), calls=%async_computation | async-start | bytes 17825792 | tf_op jit(solution)/shard_map/all_gather | solution.py:20
  299.4 36.4 %collective-permute-start.2 = (f32[128,16,128]{2,0,1:T(8,128)S(1)}, f32[128,16,128]{2,0,1:T(8,128)S(1)}, u32[]{:S(2)}, u32[]{:S(2)}) collective-permute-start(f32[128,16,128]{2,0,1:T(8,128)S(1)} %get-tuple-element.723), channel_id=1, source_target_pairs={{0,15},{1,0},{2,1},{3,2},{4,3},{5,4},{6,5},{7,6},{8,7},{9,8},{10,9... | collective-permute-start | bytes 3145736 | tf_op jit(solution)/shard_map/while/body/eval_jaxpr/ppermute | solution.py:38
  300.8 35.2 %collective-permute-start = (bf16[128,16,128]{2,0,1:T(8,128)(2,1)S(1)}, bf16[128,16,128]{2,0,1:T(8,128)(2,1)}, u32[]{:S(2)}, u32[]{:S(2)}) collective-permute-start(bf16[128,16,128]{2,0,1:T(8,128)(2,1)S(1)} %copy.169), channel_id=1, source_target_pairs={{1,0},{2,1},{3,2},{4,3},{5,4},{6,5},{7,6},{8,7},{9,8},{10,9},{11,1... | collective-permute-start | bytes 1572872 | tf_op jit(solution)/shard_map/while/body/eval_jaxpr/ppermute | solution.py:33
  304.1 31.8 %collective-permute-start.4 = (f32[16,128]{1,0:T(8,128)S(1)}, f32[16,128]{1,0:T(8,128)S(1)}, u32[]{:S(2)}, u32[]{:S(2)}) collective-permute-start(f32[16,128]{1,0:T(8,128)S(1)} %get-tuple-element.725), channel_id=1, source_target_pairs={{0,15},{1,0},{2,1},{3,2},{4,3},{5,4},{6,5},{7,6},{8,7},{9,8},{10,9... | collective-permute-start | bytes 24584 | tf_op jit(solution)/shard_map/while/body/eval_jaxpr/ppermute | solution.py:38
  305.5 30.5 %collective-permute-start.3 = (f32[16,128]{1,0:T(8,128)}, f32[16,128]{1,0:T(8,128)S(1)}, u32[]{:S(2)}, u32[]{:S(2)}) collective-permute-start(f32[16,128]{1,0:T(8,128)} %get-tuple-element.724), channel_id=1, source_target_pairs={{0,15},{1,0},{2,1},{3,2},{4,3},{5,4},{6,5},{7,6},{8,7},{9,8},{10,9... | collective-permute-start | bytes 24584 | tf_op jit(solution)/shard_map/while/body/eval_jaxpr/ppermute | solution.py:38
  306.2 29.8 %collective-permute-start.1 = (s32[128]{0:T(128)S(1)}, s32[128]{0:T(128)S(1)}, u32[]{:S(2)}, u32[]{:S(2)}) collective-permute-start(s32[128]{0:T(128)S(1)} %copy.170), channel_id=1, source_target_pairs={{1,0},{2,1},{3,2},{4,3},{5,4},{6,5},{7,6},{8,7},{9,8},{10,9},{11,1... | collective-permute-start | bytes 1544 | tf_op jit(solution)/shard_map/while/body/eval_jaxpr/ppermute | solution.py:33
  342.4 36.5 %collective-permute-start.2 = (f32[128,16,128]{2,0,1:T(8,128)S(1)}, f32[128,16,128]{2,0,1:T(8,128)S(1)}, u32[]{:S(2)}, u32[]{:S(2)}) collective-permute-start(f32[128,16,128]{2,0,1:T(8,128)S(1)} %get-tuple-element.723), channel_id=1, source_target_pairs={{0,15},{1,0},{2,1},{3,2},{4,3},{5,4},{6,5},{7,6},{8,7},{9,8},{10,9... | collective-permute-start | bytes 3145736 | tf_op jit(solution)/shard_map/while/body/eval_jaxpr/ppermute | solution.py:38
  345.9 33.2 %collective-permute-start = (bf16[128,16,128]{2,0,1:T(8,128)(2,1)S(1)}, bf16[128,16,128]{2,0,1:T(8,128)(2,1)}, u32[]{:S(2)}, u32[]{:S(2)}) collective-permute-start(bf16[128,16,128]{2,0,1:T(8,128)(2,1)S(1)} %copy.169), channel_id=1, source_target_pairs={{1,0},{2,1},{3,2},{4,3},{5,4},{6,5},{7,6},{8,7},{9,8},{10,9},{11,1... | collective-permute-start | bytes 1572872 | tf_op jit(solution)/shard_map/while/body/eval_jaxpr/ppermute | solution.py:33
  347.8 31.1 %collective-permute-start.4 = (f32[16,128]{1,0:T(8,128)S(1)}, f32[16,128]{1,0:T(8,128)S(1)}, u32[]{:S(2)}, u32[]{:S(2)}) collective-permute-start(f32[16,128]{1,0:T(8,128)S(1)} %get-tuple-element.725), channel_id=1, source_target_pairs={{0,15},{1,0},{2,1},{3,2},{4,3},{5,4},{6,5},{7,6},{8,7},{9,8},{10,9... | collective-permute-start | bytes 24584 | tf_op jit(solution)/shard_map/while/body/eval_jaxpr/ppermute | solution.py:38
  348.5 30.6 %collective-permute-start.3 = (f32[16,128]{1,0:T(8,128)}, f32[16,128]{1,0:T(8,128)S(1)}, u32[]{:S(2)}, u32[]{:S(2)}) collective-permute-start(f32[16,128]{1,0:T(8,128)} %get-tuple-element.724), channel_id=1, source_target_pairs={{0,15},{1,0},{2,1},{3,2},{4,3},{5,4},{6,5},{7,6},{8,7},{9,8},{10,9... | collective-permute-start | bytes 24584 | tf_op jit(solution)/shard_map/while/body/eval_jaxpr/ppermute | solution.py:38
  349.2 29.9 %collective-permute-start.1 = (s32[128]{0:T(128)S(1)}, s32[128]{0:T(128)S(1)}, u32[]{:S(2)}, u32[]{:S(2)}) collective-permute-start(s32[128]{0:T(128)S(1)} %copy.170), channel_id=1, source_target_pairs={{1,0},{2,1},{3,2},{4,3},{5,4},{6,5},{7,6},{8,7},{9,8},{10,9},{11,1... | collective-permute-start | bytes 1544 | tf_op jit(solution)/shard_map/while/body/eval_jaxpr/ppermute | solution.py:33
  385.5 36.8 %collective-permute-start.2 = (f32[128,16,128]{2,0,1:T(8,128)S(1)}, f32[128,16,128]{2,0,1:T(8,128)S(1)}, u32[]{:S(2)}, u32[]{:S(2)}) collective-permute-start(f32[128,16,128]{2,0,1:T(8,128)S(1)} %get-tuple-element.723), channel_id=1, source_target_pairs={{0,15},{1,0},{2,1},{3,2},{4,3},{5,4},{6,5},{7,6},{8,7},{9,8},{10,9... | collective-permute-start | bytes 3145736 | tf_op jit(solution)/shard_map/while/body/eval_jaxpr/ppermute | solution.py:38
  390.1 32.3 %collective-permute-start = (bf16[128,16,128]{2,0,1:T(8,128)(2,1)S(1)}, bf16[128,16,128]{2,0,1:T(8,128)(2,1)}, u32[]{:S(2)}, u32[]{:S(2)}) collective-permute-start(bf16[128,16,128]{2,0,1:T(8,128)(2,1)S(1)} %copy.169), channel_id=1, source_target_pairs={{1,0},{2,1},{3,2},{4,3},{5,4},{6,5},{7,6},{8,7},{9,8},{10,9},{11,1... | collective-permute-start | bytes 1572872 | tf_op jit(solution)/shard_map/while/body/eval_jaxpr/ppermute | solution.py:33
  392.0 30.2 %collective-permute-start.4 = (f32[16,128]{1,0:T(8,128)S(1)}, f32[16,128]{1,0:T(8,128)S(1)}, u32[]{:S(2)}, u32[]{:S(2)}) collective-permute-start(f32[16,128]{1,0:T(8,128)S(1)} %get-tuple-element.725), channel_id=1, source_target_pairs={{0,15},{1,0},{2,1},{3,2},{4,3},{5,4},{6,5},{7,6},{8,7},{9,8},{10,9... | collective-permute-start | bytes 24584 | tf_op jit(solution)/shard_map/while/body/eval_jaxpr/ppermute | solution.py:38
  392.1 30.3 %collective-permute-start.3 = (f32[16,128]{1,0:T(8,128)}, f32[16,128]{1,0:T(8,128)S(1)}, u32[]{:S(2)}, u32[]{:S(2)}) collective-permute-start(f32[16,128]{1,0:T(8,128)} %get-tuple-element.724), channel_id=1, source_target_pairs={{0,15},{1,0},{2,1},{3,2},{4,3},{5,4},{6,5},{7,6},{8,7},{9,8},{10,9... | collective-permute-start | bytes 24584 | tf_op jit(solution)/shard_map/while/body/eval_jaxpr/ppermute | solution.py:38
  392.5 29.9 %collective-permute-start.1 = (s32[128]{0:T(128)S(1)}, s32[128]{0:T(128)S(1)}, u32[]{:S(2)}, u32[]{:S(2)}) collective-permute-start(s32[128]{0:T(128)S(1)} %copy.170), channel_id=1, source_target_pairs={{1,0},{2,1},{3,2},{4,3},{5,4},{6,5},{7,6},{8,7},{9,8},{10,9},{11,1... | collective-permute-start | bytes 1544 | tf_op jit(solution)/shard_map/while/body/eval_jaxpr/ppermute | solution.py:33
  428.8 35.9 %collective-permute-start.2 = (f32[128,16,128]{2,0,1:T(8,128)S(1)}, f32[128,16,128]{2,0,1:T(8,128)S(1)}, u32[]{:S(2)}, u32[]{:S(2)}) collective-permute-start(f32[128,16,128]{2,0,1:T(8,128)S(1)} %get-tuple-element.723), channel_id=1, source_target_pairs={{0,15},{1,0},{2,1},{3,2},{4,3},{5,4},{6,5},{7,6},{8,7},{9,8},{10,9... | collective-permute-start | bytes 3145736 | tf_op jit(solution)/shard_map/while/body/eval_jaxpr/ppermute | solution.py:38
  433.4 31.4 %collective-permute-start = (bf16[128,16,128]{2,0,1:T(8,128)(2,1)S(1)}, bf16[128,16,128]{2,0,1:T(8,128)(2,1)}, u32[]{:S(2)}, u32[]{:S(2)}) collective-permute-start(bf16[128,16,128]{2,0,1:T(8,128)(2,1)S(1)} %copy.169), channel_id=1, source_target_pairs={{1,0},{2,1},{3,2},{4,3},{5,4},{6,5},{7,6},{8,7},{9,8},{10,9},{11,1... | collective-permute-start | bytes 1572872 | tf_op jit(solution)/shard_map/while/body/eval_jaxpr/ppermute | solution.py:33
  435.3 29.3 %collective-permute-start.4 = (f32[16,128]{1,0:T(8,128)S(1)}, f32[16,128]{1,0:T(8,128)S(1)}, u32[]{:S(2)}, u32[]{:S(2)}) collective-permute-start(f32[16,128]{1,0:T(8,128)S(1)} %get-tuple-element.725), channel_id=1, source_target_pairs={{0,15},{1,0},{2,1},{3,2},{4,3},{5,4},{6,5},{7,6},{8,7},{9,8},{10,9... | collective-permute-start | bytes 24584 | tf_op jit(solution)/shard_map/while/body/eval_jaxpr/ppermute | solution.py:38
  435.4 29.3 %collective-permute-start.3 = (f32[16,128]{1,0:T(8,128)}, f32[16,128]{1,0:T(8,128)S(1)}, u32[]{:S(2)}, u32[]{:S(2)}) collective-permute-start(f32[16,128]{1,0:T(8,128)} %get-tuple-element.724), channel_id=1, source_target_pairs={{0,15},{1,0},{2,1},{3,2},{4,3},{5,4},{6,5},{7,6},{8,7},{9,8},{10,9... | collective-permute-start | bytes 24584 | tf_op jit(solution)/shard_map/while/body/eval_jaxpr/ppermute | solution.py:38
  435.5 29.3 %collective-permute-start.1 = (s32[128]{0:T(128)S(1)}, s32[128]{0:T(128)S(1)}, u32[]{:S(2)}, u32[]{:S(2)}) collective-permute-start(s32[128]{0:T(128)S(1)} %copy.170), channel_id=1, source_target_pairs={{1,0},{2,1},{3,2},{4,3},{5,4},{6,5},{7,6},{8,7},{9,8},{10,9},{11,1... | collective-permute-start | bytes 1544 | tf_op jit(solution)/shard_map/while/body/eval_jaxpr/ppermute | solution.py:33
  471.2 34.9 %collective-permute-start.2 = (f32[128,16,128]{2,0,1:T(8,128)S(1)}, f32[128,16,128]{2,0,1:T(8,128)S(1)}, u32[]{:S(2)}, u32[]{:S(2)}) collective-permute-start(f32[128,16,128]{2,0,1:T(8,128)S(1)} %get-tuple-element.723), channel_id=1, source_target_pairs={{0,15},{1,0},{2,1},{3,2},{4,3},{5,4},{6,5},{7,6},{8,7},{9,8},{10,9... | collective-permute-start | bytes 3145736 | tf_op jit(solution)/shard_map/while/body/eval_jaxpr/ppermute | solution.py:38
  475.8 30.5 %collective-permute-start = (bf16[128,16,128]{2,0,1:T(8,128)(2,1)S(1)}, bf16[128,16,128]{2,0,1:T(8,128)(2,1)}, u32[]{:S(2)}, u32[]{:S(2)}) collective-permute-start(bf16[128,16,128]{2,0,1:T(8,128)(2,1)S(1)} %copy.169), channel_id=1, source_target_pairs={{1,0},{2,1},{3,2},{4,3},{5,4},{6,5},{7,6},{8,7},{9,8},{10,9},{11,1... | collective-permute-start | bytes 1572872 | tf_op jit(solution)/shard_map/while/body/eval_jaxpr/ppermute | solution.py:33
  477.7 28.4 %collective-permute-start.4 = (f32[16,128]{1,0:T(8,128)S(1)}, f32[16,128]{1,0:T(8,128)S(1)}, u32[]{:S(2)}, u32[]{:S(2)}) collective-permute-start(f32[16,128]{1,0:T(8,128)S(1)} %get-tuple-element.725), channel_id=1, source_target_pairs={{0,15},{1,0},{2,1},{3,2},{4,3},{5,4},{6,5},{7,6},{8,7},{9,8},{10,9... | collective-permute-start | bytes 24584 | tf_op jit(solution)/shard_map/while/body/eval_jaxpr/ppermute | solution.py:38
  477.8 28.4 %collective-permute-start.3 = (f32[16,128]{1,0:T(8,128)}, f32[16,128]{1,0:T(8,128)S(1)}, u32[]{:S(2)}, u32[]{:S(2)}) collective-permute-start(f32[16,128]{1,0:T(8,128)} %get-tuple-element.724), channel_id=1, source_target_pairs={{0,15},{1,0},{2,1},{3,2},{4,3},{5,4},{6,5},{7,6},{8,7},{9,8},{10,9... | collective-permute-start | bytes 24584 | tf_op jit(solution)/shard_map/while/body/eval_jaxpr/ppermute | solution.py:38
  477.9 28.4 %collective-permute-start.1 = (s32[128]{0:T(128)S(1)}, s32[128]{0:T(128)S(1)}, u32[]{:S(2)}, u32[]{:S(2)}) collective-permute-start(s32[128]{0:T(128)S(1)} %copy.170), channel_id=1, source_target_pairs={{1,0},{2,1},{3,2},{4,3},{5,4},{6,5},{7,6},{8,7},{9,8},{10,9},{11,1... | collective-permute-start | bytes 1544 | tf_op jit(solution)/shard_map/while/body/eval_jaxpr/ppermute | solution.py:33
  512.7 34.0 %collective-permute-start.2 = (f32[128,16,128]{2,0,1:T(8,128)S(1)}, f32[128,16,128]{2,0,1:T(8,128)S(1)}, u32[]{:S(2)}, u32[]{:S(2)}) collective-permute-start(f32[128,16,128]{2,0,1:T(8,128)S(1)} %get-tuple-element.723), channel_id=1, source_target_pairs={{0,15},{1,0},{2,1},{3,2},{4,3},{5,4},{6,5},{7,6},{8,7},{9,8},{10,9... | collective-permute-start | bytes 3145736 | tf_op jit(solution)/shard_map/while/body/eval_jaxpr/ppermute | solution.py:38
  517.3 29.5 %collective-permute-start = (bf16[128,16,128]{2,0,1:T(8,128)(2,1)S(1)}, bf16[128,16,128]{2,0,1:T(8,128)(2,1)}, u32[]{:S(2)}, u32[]{:S(2)}) collective-permute-start(bf16[128,16,128]{2,0,1:T(8,128)(2,1)S(1)} %copy.169), channel_id=1, source_target_pairs={{1,0},{2,1},{3,2},{4,3},{5,4},{6,5},{7,6},{8,7},{9,8},{10,9},{11,1... | collective-permute-start | bytes 1572872 | tf_op jit(solution)/shard_map/while/body/eval_jaxpr/ppermute | solution.py:33
  519.2 27.5 %collective-permute-start.4 = (f32[16,128]{1,0:T(8,128)S(1)}, f32[16,128]{1,0:T(8,128)S(1)}, u32[]{:S(2)}, u32[]{:S(2)}) collective-permute-start(f32[16,128]{1,0:T(8,128)S(1)} %get-tuple-element.725), channel_id=1, source_target_pairs={{0,15},{1,0},{2,1},{3,2},{4,3},{5,4},{6,5},{7,6},{8,7},{9,8},{10,9... | collective-permute-start | bytes 24584 | tf_op jit(solution)/shard_map/while/body/eval_jaxpr/ppermute | solution.py:38
  519.3 27.5 %collective-permute-start.3 = (f32[16,128]{1,0:T(8,128)}, f32[16,128]{1,0:T(8,128)S(1)}, u32[]{:S(2)}, u32[]{:S(2)}) collective-permute-start(f32[16,128]{1,0:T(8,128)} %get-tuple-element.724), channel_id=1, source_target_pairs={{0,15},{1,0},{2,1},{3,2},{4,3},{5,4},{6,5},{7,6},{8,7},{9,8},{10,9... | collective-permute-start | bytes 24584 | tf_op jit(solution)/shard_map/while/body/eval_jaxpr/ppermute | solution.py:38
  553.2 33.1 %collective-permute-start.2 = (f32[128,16,128]{2,0,1:T(8,128)S(1)}, f32[128,16,128]{2,0,1:T(8,128)S(1)}, u32[]{:S(2)}, u32[]{:S(2)}) collective-permute-start(f32[128,16,128]{2,0,1:T(8,128)S(1)} %get-tuple-element.723), channel_id=1, source_target_pairs={{0,15},{1,0},{2,1},{3,2},{4,3},{5,4},{6,5},{7,6},{8,7},{9,8},{10,9... | collective-permute-start | bytes 3145736 | tf_op jit(solution)/shard_map/while/body/eval_jaxpr/ppermute | solution.py:38
  557.8 28.6 %collective-permute-start = (bf16[128,16,128]{2,0,1:T(8,128)(2,1)S(1)}, bf16[128,16,128]{2,0,1:T(8,128)(2,1)}, u32[]{:S(2)}, u32[]{:S(2)}) collective-permute-start(bf16[128,16,128]{2,0,1:T(8,128)(2,1)S(1)} %copy.169), channel_id=1, source_target_pairs={{1,0},{2,1},{3,2},{4,3},{5,4},{6,5},{7,6},{8,7},{9,8},{10,9},{11,1... | collective-permute-start | bytes 1572872 | tf_op jit(solution)/shard_map/while/body/eval_jaxpr/ppermute | solution.py:33
  592.9 32.1 %collective-permute-start.2 = (f32[128,16,128]{2,0,1:T(8,128)S(1)}, f32[128,16,128]{2,0,1:T(8,128)S(1)}, u32[]{:S(2)}, u32[]{:S(2)}) collective-permute-start(f32[128,16,128]{2,0,1:T(8,128)S(1)} %get-tuple-element.723), channel_id=1, source_target_pairs={{0,15},{1,0},{2,1},{3,2},{4,3},{5,4},{6,5},{7,6},{8,7},{9,8},{10,9... | collective-permute-start | bytes 3145736 | tf_op jit(solution)/shard_map/while/body/eval_jaxpr/ppermute | solution.py:38
  597.5 27.6 %collective-permute-start = (bf16[128,16,128]{2,0,1:T(8,128)(2,1)S(1)}, bf16[128,16,128]{2,0,1:T(8,128)(2,1)}, u32[]{:S(2)}, u32[]{:S(2)}) collective-permute-start(bf16[128,16,128]{2,0,1:T(8,128)(2,1)S(1)} %copy.169), channel_id=1, source_target_pairs={{1,0},{2,1},{3,2},{4,3},{5,4},{6,5},{7,6},{8,7},{9,8},{10,9},{11,1... | collective-permute-start | bytes 1572872 | tf_op jit(solution)/shard_map/while/body/eval_jaxpr/ppermute | solution.py:33
  626.8 37.9 %collective-permute-start.2 = (f32[128,16,128]{2,0,1:T(8,128)S(1)}, f32[128,16,128]{2,0,1:T(8,128)S(1)}, u32[]{:S(2)}, u32[]{:S(2)}) collective-permute-start(f32[128,16,128]{2,0,1:T(8,128)S(1)} %get-tuple-element.723), channel_id=1, source_target_pairs={{0,15},{1,0},{2,1},{3,2},{4,3},{5,4},{6,5},{7,6},{8,7},{9,8},{10,9... | collective-permute-start | bytes 3145736 | tf_op jit(solution)/shard_map/while/body/eval_jaxpr/ppermute | solution.py:38
  636.2 28.7 %collective-permute-start = (bf16[128,16,128]{2,0,1:T(8,128)(2,1)S(1)}, bf16[128,16,128]{2,0,1:T(8,128)(2,1)}, u32[]{:S(2)}, u32[]{:S(2)}) collective-permute-start(bf16[128,16,128]{2,0,1:T(8,128)(2,1)S(1)} %copy.169), channel_id=1, source_target_pairs={{1,0},{2,1},{3,2},{4,3},{5,4},{6,5},{7,6},{8,7},{9,8},{10,9},{11,1... | collective-permute-start | bytes 1572872 | tf_op jit(solution)/shard_map/while/body/eval_jaxpr/ppermute | solution.py:33
  666.5 33.1 %collective-permute-start.2 = (f32[128,16,128]{2,0,1:T(8,128)S(1)}, f32[128,16,128]{2,0,1:T(8,128)S(1)}, u32[]{:S(2)}, u32[]{:S(2)}) collective-permute-start(f32[128,16,128]{2,0,1:T(8,128)S(1)} %get-tuple-element.723), channel_id=1, source_target_pairs={{0,15},{1,0},{2,1},{3,2},{4,3},{5,4},{6,5},{7,6},{8,7},{9,8},{10,9... | collective-permute-start | bytes 3145736 | tf_op jit(solution)/shard_map/while/body/eval_jaxpr/ppermute | solution.py:38
  671.1 28.7 %collective-permute-start = (bf16[128,16,128]{2,0,1:T(8,128)(2,1)S(1)}, bf16[128,16,128]{2,0,1:T(8,128)(2,1)}, u32[]{:S(2)}, u32[]{:S(2)}) collective-permute-start(bf16[128,16,128]{2,0,1:T(8,128)(2,1)S(1)} %copy.169), channel_id=1, source_target_pairs={{1,0},{2,1},{3,2},{4,3},{5,4},{6,5},{7,6},{8,7},{9,8},{10,9},{11,1... | collective-permute-start | bytes 1572872 | tf_op jit(solution)/shard_map/while/body/eval_jaxpr/ppermute | solution.py:33
  701.5 33.1 %collective-permute-start.2 = (f32[128,16,128]{2,0,1:T(8,128)S(1)}, f32[128,16,128]{2,0,1:T(8,128)S(1)}, u32[]{:S(2)}, u32[]{:S(2)}) collective-permute-start(f32[128,16,128]{2,0,1:T(8,128)S(1)} %get-tuple-element.723), channel_id=1, source_target_pairs={{0,15},{1,0},{2,1},{3,2},{4,3},{5,4},{6,5},{7,6},{8,7},{9,8},{10,9... | collective-permute-start | bytes 3145736 | tf_op jit(solution)/shard_map/while/body/eval_jaxpr/ppermute | solution.py:38
  706.1 28.7 %collective-permute-start = (bf16[128,16,128]{2,0,1:T(8,128)(2,1)S(1)}, bf16[128,16,128]{2,0,1:T(8,128)(2,1)}, u32[]{:S(2)}, u32[]{:S(2)}) collective-permute-start(bf16[128,16,128]{2,0,1:T(8,128)(2,1)S(1)} %copy.169), channel_id=1, source_target_pairs={{1,0},{2,1},{3,2},{4,3},{5,4},{6,5},{7,6},{8,7},{9,8},{10,9},{11,1... | collective-permute-start | bytes 1572872 | tf_op jit(solution)/shard_map/while/body/eval_jaxpr/ppermute | solution.py:33
  736.5 33.1 %collective-permute-start.2 = (f32[128,16,128]{2,0,1:T(8,128)S(1)}, f32[128,16,128]{2,0,1:T(8,128)S(1)}, u32[]{:S(2)}, u32[]{:S(2)}) collective-permute-start(f32[128,16,128]{2,0,1:T(8,128)S(1)} %get-tuple-element.723), channel_id=1, source_target_pairs={{0,15},{1,0},{2,1},{3,2},{4,3},{5,4},{6,5},{7,6},{8,7},{9,8},{10,9... | collective-permute-start | bytes 3145736 | tf_op jit(solution)/shard_map/while/body/eval_jaxpr/ppermute | solution.py:38
  741.1 28.7 %collective-permute-start = (bf16[128,16,128]{2,0,1:T(8,128)(2,1)S(1)}, bf16[128,16,128]{2,0,1:T(8,128)(2,1)}, u32[]{:S(2)}, u32[]{:S(2)}) collective-permute-start(bf16[128,16,128]{2,0,1:T(8,128)(2,1)S(1)} %copy.169), channel_id=1, source_target_pairs={{1,0},{2,1},{3,2},{4,3},{5,4},{6,5},{7,6},{8,7},{9,8},{10,9},{11,1... | collective-permute-start | bytes 1572872 | tf_op jit(solution)/shard_map/while/body/eval_jaxpr/ppermute | solution.py:33
  771.5 33.1 %collective-permute-start.2 = (f32[128,16,128]{2,0,1:T(8,128)S(1)}, f32[128,16,128]{2,0,1:T(8,128)S(1)}, u32[]{:S(2)}, u32[]{:S(2)}) collective-permute-start(f32[128,16,128]{2,0,1:T(8,128)S(1)} %get-tuple-element.723), channel_id=1, source_target_pairs={{0,15},{1,0},{2,1},{3,2},{4,3},{5,4},{6,5},{7,6},{8,7},{9,8},{10,9... | collective-permute-start | bytes 3145736 | tf_op jit(solution)/shard_map/while/body/eval_jaxpr/ppermute | solution.py:38
  776.1 28.7 %collective-permute-start = (bf16[128,16,128]{2,0,1:T(8,128)(2,1)S(1)}, bf16[128,16,128]{2,0,1:T(8,128)(2,1)}, u32[]{:S(2)}, u32[]{:S(2)}) collective-permute-start(bf16[128,16,128]{2,0,1:T(8,128)(2,1)S(1)} %copy.169), channel_id=1, source_target_pairs={{1,0},{2,1},{3,2},{4,3},{5,4},{6,5},{7,6},{8,7},{9,8},{10,9},{11,1... | collective-permute-start | bytes 1572872 | tf_op jit(solution)/shard_map/while/body/eval_jaxpr/ppermute | solution.py:33
  806.5 33.1 %collective-permute-start.2 = (f32[128,16,128]{2,0,1:T(8,128)S(1)}, f32[128,16,128]{2,0,1:T(8,128)S(1)}, u32[]{:S(2)}, u32[]{:S(2)}) collective-permute-start(f32[128,16,128]{2,0,1:T(8,128)S(1)} %get-tuple-element.723), channel_id=1, source_target_pairs={{0,15},{1,0},{2,1},{3,2},{4,3},{5,4},{6,5},{7,6},{8,7},{9,8},{10,9... | collective-permute-start | bytes 3145736 | tf_op jit(solution)/shard_map/while/body/eval_jaxpr/ppermute | solution.py:38
  811.1 28.7 %collective-permute-start = (bf16[128,16,128]{2,0,1:T(8,128)(2,1)S(1)}, bf16[128,16,128]{2,0,1:T(8,128)(2,1)}, u32[]{:S(2)}, u32[]{:S(2)}) collective-permute-start(bf16[128,16,128]{2,0,1:T(8,128)(2,1)S(1)} %copy.169), channel_id=1, source_target_pairs={{1,0},{2,1},{3,2},{4,3},{5,4},{6,5},{7,6},{8,7},{9,8},{10,9},{11,1... | collective-permute-start | bytes 1572872 | tf_op jit(solution)/shard_map/while/body/eval_jaxpr/ppermute | solution.py:33
  841.5 33.1 %collective-permute-start.2 = (f32[128,16,128]{2,0,1:T(8,128)S(1)}, f32[128,16,128]{2,0,1:T(8,128)S(1)}, u32[]{:S(2)}, u32[]{:S(2)}) collective-permute-start(f32[128,16,128]{2,0,1:T(8,128)S(1)} %get-tuple-element.723), channel_id=1, source_target_pairs={{0,15},{1,0},{2,1},{3,2},{4,3},{5,4},{6,5},{7,6},{8,7},{9,8},{10,9... | collective-permute-start | bytes 3145736 | tf_op jit(solution)/shard_map/while/body/eval_jaxpr/ppermute | solution.py:38
  846.1 28.7 %collective-permute-start = (bf16[128,16,128]{2,0,1:T(8,128)(2,1)S(1)}, bf16[128,16,128]{2,0,1:T(8,128)(2,1)}, u32[]{:S(2)}, u32[]{:S(2)}) collective-permute-start(bf16[128,16,128]{2,0,1:T(8,128)(2,1)S(1)} %copy.169), channel_id=1, source_target_pairs={{1,0},{2,1},{3,2},{4,3},{5,4},{6,5},{7,6},{8,7},{9,8},{10,9},{11,1... | collective-permute-start | bytes 1572872 | tf_op jit(solution)/shard_map/while/body/eval_jaxpr/ppermute | solution.py:33
  (51 other events, 878.3 us)
Sparse Core Ops, SparseCore 0:
  46.9 187.2 all-gather.3
where the time goes:
time: 924 us; the launch traced here: 911 us
  waiting for transfers between devices  538 us (58%)
  starting transfers between devices  164 us (18%)
  matrix products  114 us (12%)
  local copies, waits for them, and re-layouts  36.8 us (4%)
  other arithmetic  21.8 us (2%)
  blocking collectives  18.2 us (2%)
  between operations  14.4 us (2%)
    ppermute x48, waiting for transfers between devices, shifted(): lax.ppermute(shard, axis, [(i, (i + by) % size) for i in range(size)])  377 us
    all_gather x1, waiting for transfers between devices, entering(): pieces = lax.all_gather(value, axis)  161 us
    ppermute x48, starting transfers between devices, shifted(): lax.ppermute(shard, axis, [(i, (i + by) % size) for i in range(size)])  83.4 us
    ppermute x32, starting transfers between devices, from_behind(): lax.ppermute(value, axis, [(source, source + steps) for source in range(i...  80.8 us
    dot_general x17, matrix products, compose(): return jnp.einsum('hij,hjk->hik', earlier, following, precision=highest)  49.7 us
    while x93, local copies, waits for them, and re-layouts  23.7 us
  transfers between devices with their start and end apart: 81, of which 24 were waited for; matrix products, arithmetic and copies ran while one was open for 1% of the time, Pallas kernels for 0%

commit v1 on v0

v1 whole, which is shorter than its diff:
```python
import functools
import math

import jax
import jax.numpy as jnp
from jax import lax
from jax.experimental import pallas as pl
from jax.experimental.pallas import tpu as pltpu
from jax.sharding import PartitionSpec as P

HEADS = 16
HD = 128
TOK = 128
LENGTH = 2048
BAND = 1024
ROWS = 256
SPAN = BAND + ROWS
BLOCKS = LENGTH // TOK
GROUP = 4
EPSILON = 1e-06
FAR = 2.0**100
F32 = jnp.float32
BF16 = jnp.bfloat16
MESH = pl.DeviceIdType.MESH


def dot(a, b):
    return lax.dot_general(a, b, (((1,), (0,)), ((), ())), preferred_element_type=F32)


def dot_nt(a, b):
    return lax.dot_general(a, b, (((1,), (1,)), ((), ())), preferred_element_type=F32)


def dot_tn(a, b):
    return lax.dot_general(a, b, (((0,), (0,)), ((), ())), preferred_element_type=F32)


def halves(x):
    high = x.astype(BF16)
    return high, (x - high.astype(F32)).astype(BF16)


def beside(a, b):
    return jnp.concatenate([a, b], axis=1)


def below(a, b):
    return jnp.concatenate([a, b], axis=0)


def product(a_high, a_low, b_high, b_low):
    return dot(beside(a_high, a_low), below(b_high, b_high)) + dot(a_high, b_low)


def at_block(index, size=TOK):
    return pl.ds(pl.multiple_of(index * size, size), size)


def square_iota():
    i = lax.broadcasted_iota(jnp.int32, (TOK, TOK), 0)
    j = lax.broadcasted_iota(jnp.int32, (TOK, TOK), 1)
    return i, j


def merge_reflections(r_buf, y_buf):
    i, j = square_iota()
    apart = jnp.bitwise_xor(i, j)

    def group(g, carry):
        raws, merged, betas = [], [], []
        for u in range(GROUP):
            raw = r_buf[at_block(g * GROUP + u), :]
            wide = raw.astype(F32)
            beta = 2.0 / (jnp.sum(wide * wide, axis=1, keepdims=True) + EPSILON)
            raws.append(raw)
            betas.append(beta)
            merged.append(wide * beta)
        for level in range(7):
            chosen = (lax.shift_right_logical(apart, level) == 1) & (i > j)
            for u in range(GROUP):
                raw = raws[u]
                high, low = halves(merged[u])
                if level == 0:
                    cross = dot_nt(raw, raw) * betas[u]
                else:
                    cross = dot_nt(beside(high, low), beside(raw, raw))
                c_high, c_low = halves(jnp.where(chosen, cross, 0.0))
                merged[u] = merged[u] - product(c_high, c_low, high, low)
        for u in range(GROUP):
            y_buf[at_block(g * GROUP + u), :] = merged[u]
        return carry

    lax.fori_loop(0, BLOCKS // GROUP, group, 0)


def chain_blocks(r_buf, y_buf, w_buf):
    i, j = square_iota()

    def step(b, before):
        raw = r_buf[at_block(b), :]
        a_high, a_low = halves(before)
        y_high, y_low = halves(y_buf[at_block(b), :])
        z_high, z_low = halves(product(y_high, y_low, a_high, a_low))
        w_buf[b, :TOK, :TOK] = a_high
        w_buf[b, :TOK, TOK:] = a_low
        w_buf[b, TOK:, :TOK] = -z_high
        w_buf[b, TOK:, TOK:] = -z_low
        return before - dot_tn(below(raw, raw), below(z_high, z_low))

    lax.fori_loop(0, BLOCKS, step, jnp.where(i == j, 1.0, 0.0).astype(F32))


def rotate(x_buf, r_buf, w_buf, put):
    i, j = square_iota()

    def some(g, carry):
        for u in range(GROUP):
            b = g * GROUP + u
            raw_x = x_buf[at_block(b), :]
            seen = jnp.where(i >= j, dot_nt(raw_x, r_buf[at_block(b), :]), 0.0)
            s_high, s_low = halves(seen)
            both = dot(beside(raw_x, s_high), w_buf[b])
            rest = dot(s_low, w_buf[b, TOK:, :TOK])
            put(b, (both[:, :TOK] + both[:, TOK:] + rest).astype(BF16))
        return carry

    lax.fori_loop(0, BLOCKS // GROUP, some, 0)


def place_documents(segments, q_full, k_full):
    i, _ = square_iota()

    def one(b, carry):
        hot = jnp.where(segments[b] == i, 1.0, 0.0).astype(F32).T
        q_full[at_block(b), TOK:] = (hot * FAR).astype(BF16)
        k_full[pl.ds(pl.multiple_of(BAND + b * TOK, TOK), TOK), TOK:] = (hot - 1.0).astype(BF16)
        return carry

    lax.fori_loop(0, BLOCKS, one, 0)


def prepare_bands(k_full, v_full):
    k_full[:BAND, :TOK] = jnp.zeros((BAND, TOK), BF16)
    k_full[:BAND, TOK:] = jnp.full((BAND, TOK), -1.0, BF16)
    v_full[:BAND, :TOK] = jnp.zeros((BAND, TOK), BF16)
    v_full[:, TOK:] = jnp.ones((BAND + LENGTH, TOK), BF16)


def weigh(q_full, k_full, s_buf, p_buf):
    i = lax.broadcasted_iota(jnp.int32, (ROWS, ROWS), 0)
    j = lax.broadcasted_iota(jnp.int32, (ROWS, ROWS), 1)
    scale = math.log2(math.e) / math.sqrt(HD)

    def tile(t, carry):
        q_rows = q_full[at_block(t, ROWS), :]
        most = None
        for n in range(SPAN // ROWS):
            keys = k_full[pl.ds(pl.multiple_of((t + n) * ROWS, ROWS), ROWS), :]
            scores = dot_nt(q_rows, keys)
            if n == SPAN // ROWS - 1:
                scores = jnp.where(i >= j, scores, -FAR)
            s_buf[:, n * ROWS : (n + 1) * ROWS] = scores
            folded = jnp.maximum(scores[:, :TOK], scores[:, TOK:])
            most = folded if most is None else jnp.maximum(most, folded)
        top = jnp.max(most, axis=1, keepdims=True)
        for n in range(SPAN // ROWS):
            piece = slice(n * ROWS, (n + 1) * ROWS)
            p_buf[t, :, piece] = jnp.exp2((s_buf[:, piece] - top) * scale).astype(BF16)
        return carry

    lax.fori_loop(0, LENGTH // ROWS, tile, 0)


def mix(t, p_buf, v_full, gains, o_buf):
    both = dot(p_buf[t], v_full[pl.ds(pl.multiple_of(t * ROWS, ROWS), SPAN), :])
    o_buf[at_block(t, ROWS), :] = (both[:, :TOK] / both[:, TOK:] * gains[...]).astype(BF16)


def kernel(
    q_in, k_in, v_in, r_in, segment_in, gain_in, out,
    r_buf, q_buf, k_buf, v_full, segments, gains,
    y_buf, w_buf, q_full, k_full, s_buf, p_buf, o_buf,
    send_sem, recv_sem, own_sem, out_send, out_recv, out_own, gain_send, gain_recv, gain_own,
):
    row, me = lax.axis_index("dp"), lax.axis_index("ctx")
    count = BLOCKS
    crossed = {"dp": me, "ctx": row}
    away = row != me

    def partner(d):
        return lax.rem(me + d, count)

    def source(a, t):
        if a == 4:
            return segment_in
        return (r_in, q_in, k_in, v_in)[a].at[0, :, at_block(t)]

    def target(a):
        if a == 4:
            return segments.at[me]
        if a == 3:
            return v_full.at[pl.ds(pl.multiple_of(BAND + me * TOK, TOK), TOK), pl.ds(0, TOK)]
        return (r_buf, q_buf, k_buf)[a].at[at_block(me), :]

    def remote(a, d):
        t = partner(d)
        return pltpu.make_async_remote_copy(
            src_ref=source(a, t), dst_ref=target(a), send_sem=send_sem.at[a, d], recv_sem=recv_sem.at[a, d],
            device_id={"ctx": t}, device_id_type=MESH,
        )

    def own(a):
        return pltpu.make_async_copy(source(a, me), target(a), own_sem.at[a])

    def gain_copy():
        return pltpu.make_async_remote_copy(
            src_ref=gain_in, dst_ref=gains, send_sem=gain_send, recv_sem=gain_recv,
            device_id=crossed, device_id_type=MESH,
        )

    def each_partner(act):
        def one(d, carry):
            act(d)
            return carry

        lax.fori_loop(1, count, one, 0)

    def arrive(a):
        own(a).wait()
        each_partner(lambda d: remote(a, d).wait_recv())

    for a in range(5):
        own(a).start()
    barrier = pltpu.get_barrier_semaphore()
    each_partner(
        lambda d: pl.semaphore_signal(barrier, inc=1, device_id={"ctx": partner(d)}, device_id_type=MESH)
    )

    @pl.when(away)
    def _():
        pl.semaphore_signal(barrier, inc=1, device_id=crossed, device_id_type=MESH)

    pl.semaphore_wait(barrier, jnp.where(away, count, count - 1))

    for a in (0, 4, 1, 2, 3):
        each_partner(lambda d, a=a: remote(a, d).start())

    @pl.when(away)
    def _():
        gain_copy().start()

    @pl.when(jnp.logical_not(away))
    def _():
        pltpu.make_async_copy(gain_in, gains, gain_own).start()

    prepare_bands(k_full, v_full)
    arrive(0)
    merge_reflections(r_buf, y_buf)
    chain_blocks(r_buf, y_buf, w_buf)
    arrive(4)
    place_documents(segments, q_full, k_full)
    arrive(1)

    def put_query(b, rows):
        q_full[at_block(b), :TOK] = rows

    def put_key(b, rows):
        k_full[pl.ds(pl.multiple_of(BAND + b * TOK, TOK), TOK), :TOK] = rows

    rotate(q_buf, r_buf, w_buf, put_query)
    arrive(2)
    rotate(k_buf, r_buf, w_buf, put_key)
    weigh(q_full, k_full, s_buf, p_buf)

    @pl.when(away)
    def _():
        gain_copy().wait()

    @pl.when(jnp.logical_not(away))
    def _():
        pltpu.make_async_copy(gain_in, gains, gain_own).wait()

    arrive(3)

    def out_copy(t):
        return pltpu.make_async_remote_copy(
            src_ref=o_buf.at[at_block(t), :], dst_ref=out.at[0, :, at_block(me)],
            send_sem=out_send.at[t], recv_sem=out_recv.at[me], device_id={"ctx": t}, device_id_type=MESH,
        )

    def out_own_copy():
        return pltpu.make_async_copy(o_buf.at[at_block(me), :], out.at[0, :, at_block(me)], out_own)

    def finish(n, carry):
        tile = lax.rem(me // 2 + n, LENGTH // ROWS)
        mix(tile, p_buf, v_full, gains, o_buf)
        for half in range(ROWS // TOK):
            t = tile * (ROWS // TOK) + half

            @pl.when(t != me)
            def _():
                out_copy(t).start()

            @pl.when(t == me)
            def _():
                out_own_copy().start()

        return carry

    lax.fori_loop(0, LENGTH // ROWS, finish, 0)

    for a in range(5):
        each_partner(lambda d, a=a: remote(a, d).wait_send())
    each_partner(lambda d: out_copy(partner(d)).wait_send())

    def out_arrived(d):
        s = partner(d)
        pltpu.make_async_remote_copy(
            src_ref=o_buf.at[at_block(s), :], dst_ref=out.at[0, :, at_block(s)],
            send_sem=out_send.at[s], recv_sem=out_recv.at[s], device_id={"ctx": s}, device_id_type=MESH,
        ).wait_recv()

    each_partner(out_arrived)
    out_own_copy().wait()


def local(queries, key_rows, value_rows, reflections, segment_ids, head_gains):
    hbm = pl.BlockSpec(memory_space=pltpu.HBM)
    vmem = pl.BlockSpec(memory_space=pltpu.VMEM)
    dma = pltpu.SemaphoreType.DMA
    return pl.pallas_call(
        kernel,
        out_shape=jax.ShapeDtypeStruct((1, TOK, HEADS * HD), BF16),
        in_specs=[hbm, hbm, hbm, hbm, vmem, vmem],
        out_specs=hbm,
        scratch_shapes=[
            pltpu.VMEM((LENGTH, HD), BF16),
            pltpu.VMEM((LENGTH, HD), BF16),
            pltpu.VMEM((LENGTH, HD), BF16),
            pltpu.VMEM((BAND + LENGTH, 2 * HD), BF16),
            pltpu.VMEM((BLOCKS, 1, TOK), jnp.int32),
            pltpu.VMEM((1, HD), F32),
            pltpu.VMEM((LENGTH, HD), F32),
            pltpu.VMEM((BLOCKS, 2 * HD, 2 * HD), BF16),
            pltpu.VMEM((LENGTH, 2 * HD), BF16),
            pltpu.VMEM((BAND + LENGTH, 2 * HD), BF16),
            pltpu.VMEM((ROWS, SPAN), F32),
            pltpu.VMEM((LENGTH // ROWS, ROWS, SPAN), BF16),
            pltpu.VMEM((LENGTH, HD), BF16),
            dma((5, BLOCKS)),
            dma((5, BLOCKS)),
            dma((5,)),
            dma((BLOCKS,)),
            dma((BLOCKS,)),
            dma,
            dma,
            dma,
            dma,
        ],
        compiler_params=pltpu.CompilerParams(
            collective_id=0, has_side_effects=True, vmem_limit_bytes=63 * 1024 * 1024
        ),
    )(queries, key_rows, value_rows, reflections, segment_ids, head_gains[None, :])


def solution(mesh):
    placed = (
        P("dp", "ctx", None),
        P("dp", "ctx", None),
        P("dp", "ctx", None),
        P("dp", "ctx", None),
        P("dp", "ctx"),
        P("dp"),
    )
    return jax.shard_map(
        local, mesh=mesh, in_specs=placed, out_specs=P("dp", "ctx", None), check_vma=False
    )
```

time: 924 us -> 78 us (0.08)
  the two profiles are of different devices: /device:TPU:30 before, /device:TPU:8 now
where the time goes in v1:
time: 78 us; the launch traced here: 77.8 us
  Pallas kernels  75.9 us (97%)
  local copies, waits for them, and re-layouts  1.88 us (2%)
    pallas_call x1, Pallas kernels, local(): pl.pallas_call(kernel, out_shape=jax.ShapeDtypeStruct((1, TOK, HEADS * HD...  75.9 us
    unnamed x1, local copies, waits for them, and re-layouts  1.88 us

profile of v1, /device:TPU:8, one launch (start us, length us, event | category | flops | bytes accessed | tf_op | source)
XLA Modules:
  0.0 77.8 jit_solution(14639663625473615661)
XLA Ops:
  0.0 75.9 %shard_map.64 = bf16[1,128,2048]{2,1,0:T(8,128)(2,1)} custom-call(bf16[1,128,2048]{2,1,0:T(8,128)(2,1)} %q_in.1, bf16[1,128,2048]{2,1,0:T(8,128)(2,1)} %k_in.1, bf16[1,128,2048]{2,1,0:T(8,128)(2,1)} %v_in.1, bf16[1,128,2048]{2,1,0:T(8,128)(2,1)} %r_in.1, s32[1,128]{1,0:T(1,128)} %segment_in.1, f32[1,128]{1,0:T(1,128)} %bitcast.1), custom_call_target="tpu_custom_call" | custom-call | tf_op jit(solution)/shard_map/pallas_call | solution.py:332
  76.0 1.9 %copy.8 = bf16[1,128,2048]{2,1,0:T(8,128)(2,1)} copy(bf16[1,128,2048]{2,1,0:T(8,128)(2,1)} %shard_map.64) | data formatting | bytes 1048576

commit v2 on v1

--- a/solution.py
+++ b/solution.py
@@ -243,16 +243,16 @@
 
     pl.semaphore_wait(barrier, jnp.where(away, count, count - 1))
 
-    for a in (0, 4, 1, 2, 3):
+    @pl.when(away)
+    def _():
+        gain_copy().start()
+
+    @pl.when(jnp.logical_not(away))
+    def _():
+        pltpu.make_async_copy(gain_in, gains, gain_own).start()
+
+    for a in (4, 0, 1, 2, 3):
         each_partner(lambda d, a=a: remote(a, d).start())
-
-    @pl.when(away)
-    def _():
-        gain_copy().start()
-
-    @pl.when(jnp.logical_not(away))
-    def _():
-        pltpu.make_async_copy(gain_in, gains, gain_own).start()
 
     prepare_bands(k_full, v_full)
     arrive(0)
@@ -293,7 +293,7 @@
         return pltpu.make_async_copy(o_buf.at[at_block(me), :], out.at[0, :, at_block(me)], out_own)
 
     def finish(n, carry):
-        tile = lax.rem(me // 2 + n, LENGTH // ROWS)
+        tile = lax.rem(me // 2 + n + 1, LENGTH // ROWS)
         mix(tile, p_buf, v_full, gains, o_buf)
         for half in range(ROWS // TOK):
             t = tile * (ROWS // TOK) + half
@@ -331,9 +331,9 @@
     dma = pltpu.SemaphoreType.DMA
     return pl.pallas_call(
         kernel,
-        out_shape=jax.ShapeDtypeStruct((1, TOK, HEADS * HD), BF16),
+        out_shape=pltpu.VMEM((1, TOK, HEADS * HD), BF16),
         in_specs=[hbm, hbm, hbm, hbm, vmem, vmem],
-        out_specs=hbm,
+        out_specs=pl.BlockSpec(memory_space=pl.ANY),
         scratch_shapes=[
             pltpu.VMEM((LENGTH, HD), BF16),
             pltpu.VMEM((LENGTH, HD), BF16),

time: 78 us -> 74 us (0.949)
  the two profiles are of different devices: /device:TPU:8 before, /device:TPU:6 now
where the time goes in v2:
time: 74 us; the launch traced here: 73.8 us
  Pallas kernels  73 us (99%)
  local copies, waits for them, and re-layouts  0.8 us (1%)
    pallas_call x1, Pallas kernels, local(): pl.pallas_call(kernel, out_shape=pltpu.VMEM((1, TOK, HEADS * HD), BF16),...  73 us

profile of v2, /device:TPU:6, one launch (start us, length us, event | category | flops | bytes accessed | tf_op | source)
XLA Modules:
  0.0 73.8 jit_solution(1690315772424347416)
XLA Ops:
  0.0 73.0 %shard_map.64 = bf16[1,128,2048]{2,1,0:T(8,128)(2,1)S(1)} custom-call(bf16[1,128,2048]{2,1,0:T(8,128)(2,1)} %q_in.1, bf16[1,128,2048]{2,1,0:T(8,128)(2,1)} %k_in.1, bf16[1,128,2048]{2,1,0:T(8,128)(2,1)} %v_in.1, bf16[1,128,2048]{2,1,0:T(8,128)(2,1)} %r_in.1, s32[1,128]{1,0:T(1,128)} %segment_in.1, f32[1,128]{1,0:T(1,128)} %bitcast.1), custom_call_target="tpu_custom_call" | custom-call | tf_op jit(solution)/shard_map/pallas_call | solution.py:332
  73.0 0.8 %copy.8 = bf16[1,128,2048]{2,1,0:T(8,128)(2,1)} copy(bf16[1,128,2048]{2,1,0:T(8,128)(2,1)S(1)} %shard_map.64) | data formatting | bytes 1048576

commit v3 on v2

--- a/solution.py
+++ b/solution.py
@@ -111,21 +111,15 @@
     lax.fori_loop(0, BLOCKS, step, jnp.where(i == j, 1.0, 0.0).astype(F32))
 
 
-def rotate(x_buf, r_buf, w_buf, put):
+def rotate(blocks, x_buf, r_buf, w_buf, put):
     i, j = square_iota()
-
-    def some(g, carry):
-        for u in range(GROUP):
-            b = g * GROUP + u
-            raw_x = x_buf[at_block(b), :]
-            seen = jnp.where(i >= j, dot_nt(raw_x, r_buf[at_block(b), :]), 0.0)
-            s_high, s_low = halves(seen)
-            both = dot(beside(raw_x, s_high), w_buf[b])
-            rest = dot(s_low, w_buf[b, TOK:, :TOK])
-            put(b, (both[:, :TOK] + both[:, TOK:] + rest).astype(BF16))
-        return carry
-
-    lax.fori_loop(0, BLOCKS // GROUP, some, 0)
+    for b in blocks:
+        raw_x = x_buf[at_block(b), :]
+        seen = jnp.where(i >= j, dot_nt(raw_x, r_buf[at_block(b), :]), 0.0)
+        s_high, s_low = halves(seen)
+        both = dot(beside(raw_x, s_high), w_buf[b])
+        rest = dot(s_low, w_buf[b, TOK:, :TOK])
+        put(b, (both[:, :TOK] + both[:, TOK:] + rest).astype(BF16))
 
 
 def place_documents(segments, q_full, k_full):
@@ -147,33 +141,28 @@
     v_full[:, TOK:] = jnp.ones((BAND + LENGTH, TOK), BF16)
 
 
-def weigh(q_full, k_full, s_buf, p_buf):
+def weigh(t, q_full, k_full, s_buf, p_buf):
     i = lax.broadcasted_iota(jnp.int32, (ROWS, ROWS), 0)
     j = lax.broadcasted_iota(jnp.int32, (ROWS, ROWS), 1)
     scale = math.log2(math.e) / math.sqrt(HD)
-
-    def tile(t, carry):
-        q_rows = q_full[at_block(t, ROWS), :]
-        most = None
-        for n in range(SPAN // ROWS):
-            keys = k_full[pl.ds(pl.multiple_of((t + n) * ROWS, ROWS), ROWS), :]
-            scores = dot_nt(q_rows, keys)
-            if n == SPAN // ROWS - 1:
-                scores = jnp.where(i >= j, scores, -FAR)
-            s_buf[:, n * ROWS : (n + 1) * ROWS] = scores
-            folded = jnp.maximum(scores[:, :TOK], scores[:, TOK:])
-            most = folded if most is None else jnp.maximum(most, folded)
-        top = jnp.max(most, axis=1, keepdims=True)
-        for n in range(SPAN // ROWS):
-            piece = slice(n * ROWS, (n + 1) * ROWS)
-            p_buf[t, :, piece] = jnp.exp2((s_buf[:, piece] - top) * scale).astype(BF16)
-        return carry
-
-    lax.fori_loop(0, LENGTH // ROWS, tile, 0)
+    q_rows = q_full[at_block(t, ROWS), :]
+    most = None
+    for n in range(SPAN // ROWS):
+        keys = k_full[pl.ds(pl.multiple_of((t + n) * ROWS, ROWS), ROWS), :]
+        scores = dot_nt(q_rows, keys)
+        if n == SPAN // ROWS - 1:
+            scores = jnp.where(i >= j, scores, -FAR)
+        s_buf[:, n * ROWS : (n + 1) * ROWS] = scores
+        folded = jnp.maximum(scores[:, :TOK], scores[:, TOK:])
+        most = folded if most is None else jnp.maximum(most, folded)
+    top = jnp.max(most, axis=1, keepdims=True)
+    for n in range(SPAN // ROWS):
+        piece = slice(n * ROWS, (n + 1) * ROWS)
+        p_buf[:, piece] = jnp.exp2((s_buf[:, piece] - top) * scale).astype(BF16)
 
 
 def mix(t, p_buf, v_full, gains, o_buf):
-    both = dot(p_buf[t], v_full[pl.ds(pl.multiple_of(t * ROWS, ROWS), SPAN), :])
+    both = dot(p_buf[...], v_full[pl.ds(pl.multiple_of(t * ROWS, ROWS), SPAN), :])
     o_buf[at_block(t, ROWS), :] = (both[:, :TOK] / both[:, TOK:] * gains[...]).astype(BF16)
 
 
@@ -188,8 +177,11 @@
     crossed = {"dp": me, "ctx": row}
     away = row != me
 
+    tiles = LENGTH // ROWS
+    pair, half = me // 2, lax.rem(me, 2)
+
     def partner(d):
-        return lax.rem(me + d, count)
+        return 2 * lax.rem(pair + d // 2, tiles) + lax.rem(half + d, 2)
 
     def source(a, t):
         if a == 4:
@@ -251,7 +243,7 @@
     def _():
         pltpu.make_async_copy(gain_in, gains, gain_own).start()
 
-    for a in (4, 0, 1, 2, 3):
+    for a in (4, 0, 2, 3, 1):
         each_partner(lambda d, a=a: remote(a, d).start())
 
     prepare_bands(k_full, v_full)
@@ -260,7 +252,7 @@
     chain_blocks(r_buf, y_buf, w_buf)
     arrive(4)
     place_documents(segments, q_full, k_full)
-    arrive(1)
+    arrive(2)
 
     def put_query(b, rows):
         q_full[at_block(b), :TOK] = rows
@@ -268,10 +260,11 @@
     def put_key(b, rows):
         k_full[pl.ds(pl.multiple_of(BAND + b * TOK, TOK), TOK), :TOK] = rows
 
-    rotate(q_buf, r_buf, w_buf, put_query)
-    arrive(2)
-    rotate(k_buf, r_buf, w_buf, put_key)
-    weigh(q_full, k_full, s_buf, p_buf)
+    def some_keys(g, carry):
+        rotate([g * GROUP + u for u in range(GROUP)], k_buf, r_buf, w_buf, put_key)
+        return carry
+
+    lax.fori_loop(0, BLOCKS // GROUP, some_keys, 0)
 
     @pl.when(away)
     def _():
@@ -292,23 +285,27 @@
     def out_own_copy():
         return pltpu.make_async_copy(o_buf.at[at_block(me), :], out.at[0, :, at_block(me)], out_own)
 
+    def attend(tile):
+        rotate([2 * tile, 2 * tile + 1], q_buf, r_buf, w_buf, put_query)
+        weigh(tile, q_full, k_full, s_buf, p_buf)
+        mix(tile, p_buf, v_full, gains, o_buf)
+
+    own(1).wait()
+    remote(1, 1).wait_recv()
+    attend(pair)
+    out_own_copy().start()
+    out_copy(partner(1)).start()
+
     def finish(n, carry):
-        tile = lax.rem(me // 2 + n + 1, LENGTH // ROWS)
-        mix(tile, p_buf, v_full, gains, o_buf)
-        for half in range(ROWS // TOK):
-            t = tile * (ROWS // TOK) + half
-
-            @pl.when(t != me)
-            def _():
-                out_copy(t).start()
-
-            @pl.when(t == me)
-            def _():
-                out_own_copy().start()
-
+        tile = lax.rem(pair + tiles - n, tiles)
+        remote(1, 2 * n).wait_recv()
+        remote(1, 2 * n + 1).wait_recv()
+        attend(tile)
+        for h in range(2):
+            out_copy(2 * tile + h).start()
         return carry
 
-    lax.fori_loop(0, LENGTH // ROWS, finish, 0)
+    lax.fori_loop(1, tiles, finish, 0)
 
     for a in range(5):
         each_partner(lambda d, a=a: remote(a, d).wait_send())
@@ -346,7 +343,7 @@
             pltpu.VMEM((LENGTH, 2 * HD), BF16),
             pltpu.VMEM((BAND + LENGTH, 2 * HD), BF16),
             pltpu.VMEM((ROWS, SPAN), F32),
-            pltpu.VMEM((LENGTH // ROWS, ROWS, SPAN), BF16),
+            pltpu.VMEM((ROWS, SPAN), BF16),
             pltpu.VMEM((LENGTH, HD), BF16),
             dma((5, BLOCKS)),
             dma((5, BLOCKS)),

time: 74 us -> 71.9 us (0.972)
  Pallas kernels: 73 us -> 71 us
    pallas_call x1, Pallas kernels: 73 us -> 71 us  [local(): pl.pallas_call(kernel, out_shape=pltpu.VMEM((1, TOK, HEADS * HD), BF16),...]
where the time goes in v3:
time: 71.9 us
  Pallas kernels  71 us (99%)
  local copies, waits for them, and re-layouts  0.8 us (1%)
    pallas_call x1, Pallas kernels, local(): pl.pallas_call(kernel, out_shape=pltpu.VMEM((1, TOK, HEADS * HD), BF16),...  71 us

profile of v3, /device:TPU:6, one launch (start us, length us, event | category | flops | bytes accessed | tf_op | source)
XLA Modules:
  0.0 71.9 jit_solution(17604497636778613217)
XLA Ops:
  0.0 71.0 %shard_map.64 = bf16[1,128,2048]{2,1,0:T(8,128)(2,1)S(1)} custom-call(bf16[1,128,2048]{2,1,0:T(8,128)(2,1)} %q_in.1, bf16[1,128,2048]{2,1,0:T(8,128)(2,1)} %k_in.1, bf16[1,128,2048]{2,1,0:T(8,128)(2,1)} %v_in.1, bf16[1,128,2048]{2,1,0:T(8,128)(2,1)} %r_in.1, s32[1,128]{1,0:T(1,128)} %segment_in.1, f32[1,128]{1,0:T(1,128)} %bitcast.1), custom_call_target="tpu_custom_call" | custom-call | tf_op jit(solution)/shard_map/pallas_call | solution.py:329
  71.1 0.8 %copy.8 = bf16[1,128,2048]{2,1,0:T(8,128)(2,1)} copy(bf16[1,128,2048]{2,1,0:T(8,128)(2,1)S(1)} %shard_map.64) | data formatting | bytes 1048576

commit v4 on v3

--- a/solution.py
+++ b/solution.py
@@ -170,7 +170,7 @@
     q_in, k_in, v_in, r_in, segment_in, gain_in, out,
     r_buf, q_buf, k_buf, v_full, segments, gains,
     y_buf, w_buf, q_full, k_full, s_buf, p_buf, o_buf,
-    send_sem, recv_sem, own_sem, out_send, out_recv, out_own, gain_send, gain_recv, gain_own,
+    send_sem, recv_sem, own_sem, q_send, q_recv, out_send, out_recv, out_own, gain_send, gain_recv, gain_own,
 ):
     row, me = lax.axis_index("dp"), lax.axis_index("ctx")
     count = BLOCKS
@@ -184,26 +184,56 @@
         return 2 * lax.rem(pair + d // 2, tiles) + lax.rem(half + d, 2)
 
     def source(a, t):
-        if a == 4:
+        if a == 3:
             return segment_in
-        return (r_in, q_in, k_in, v_in)[a].at[0, :, at_block(t)]
+        return (r_in, k_in, v_in)[a].at[0, :, at_block(t)]
 
     def target(a):
-        if a == 4:
+        if a == 3:
             return segments.at[me]
-        if a == 3:
+        if a == 2:
             return v_full.at[pl.ds(pl.multiple_of(BAND + me * TOK, TOK), TOK), pl.ds(0, TOK)]
-        return (r_buf, q_buf, k_buf)[a].at[at_block(me), :]
+        return (r_buf, k_buf)[a].at[at_block(me), :]
 
     def remote(a, d):
         t = partner(d)
         return pltpu.make_async_remote_copy(
-            src_ref=source(a, t), dst_ref=target(a), send_sem=send_sem.at[a, d], recv_sem=recv_sem.at[a, d],
+            src_ref=source(a, t), dst_ref=target(a), send_sem=send_sem.at[a], recv_sem=recv_sem.at[a],
             device_id={"ctx": t}, device_id_type=MESH,
+        )
+
+    def all_of(a):
+        rows = pl.ds(0, LENGTH - TOK)
+        if a == 3:
+            whole = segments.at[pl.ds(0, count - 1)]
+        elif a == 2:
+            whole = v_full.at[rows, pl.ds(0, TOK)]
+        else:
+            whole = (r_buf, k_buf)[a].at[rows, :]
+        return pltpu.make_async_remote_copy(
+            src_ref=whole, dst_ref=whole, send_sem=send_sem.at[a], recv_sem=recv_sem.at[a],
+            device_id={"ctx": partner(1)}, device_id_type=MESH,
+        )
+
+    def query(d):
+        t = partner(d)
+        return pltpu.make_async_remote_copy(
+            src_ref=q_in.at[0, :, at_block(t)], dst_ref=q_buf.at[at_block(me), :],
+            send_sem=q_send, recv_sem=q_recv.at[d // 2], device_id={"ctx": t}, device_id_type=MESH,
+        )
+
+    def some_queries(n, rows):
+        whole = q_buf.at[pl.ds(0, rows), :]
+        return pltpu.make_async_remote_copy(
+            src_ref=whole, dst_ref=whole, send_sem=q_send, recv_sem=q_recv.at[n],
+            device_id={"ctx": partner(1)}, device_id_type=MESH,
         )
 
     def own(a):
         return pltpu.make_async_copy(source(a, me), target(a), own_sem.at[a])
+
+    def own_query():
+        return pltpu.make_async_copy(q_in.at[0, :, at_block(me)], q_buf.at[at_block(me), :], own_sem.at[4])
 
     def gain_copy():
         return pltpu.make_async_remote_copy(
@@ -220,19 +250,19 @@
 
     def arrive(a):
         own(a).wait()
-        each_partner(lambda d: remote(a, d).wait_recv())
-
-    for a in range(5):
-        own(a).start()
+        all_of(a).wait_recv()
+
     barrier = pltpu.get_barrier_semaphore()
-    each_partner(
-        lambda d: pl.semaphore_signal(barrier, inc=1, device_id={"ctx": partner(d)}, device_id_type=MESH)
-    )
 
     @pl.when(away)
     def _():
         pl.semaphore_signal(barrier, inc=1, device_id=crossed, device_id_type=MESH)
 
+    for d in range(1, count):
+        pl.semaphore_signal(barrier, inc=1, device_id={"ctx": partner(d)}, device_id_type=MESH)
+    for a in range(4):
+        own(a).start()
+    own_query().start()
     pl.semaphore_wait(barrier, jnp.where(away, count, count - 1))
 
     @pl.when(away)
@@ -243,16 +273,19 @@
     def _():
         pltpu.make_async_copy(gain_in, gains, gain_own).start()
 
-    for a in (4, 0, 2, 3, 1):
+    for a in (0, 3, 1, 2):
         each_partner(lambda d, a=a: remote(a, d).start())
+    each_partner(lambda d: query(d).start())
 
     prepare_bands(k_full, v_full)
     arrive(0)
     merge_reflections(r_buf, y_buf)
     chain_blocks(r_buf, y_buf, w_buf)
-    arrive(4)
+    arrive(3)
+    all_of(0).wait_send()
     place_documents(segments, q_full, k_full)
-    arrive(2)
+    arrive(1)
+    all_of(3).wait_send()
 
     def put_query(b, rows):
         q_full[at_block(b), :TOK] = rows
@@ -274,12 +307,13 @@
     def _():
         pltpu.make_async_copy(gain_in, gains, gain_own).wait()
 
-    arrive(3)
+    arrive(2)
+    all_of(1).wait_send()
 
     def out_copy(t):
         return pltpu.make_async_remote_copy(
             src_ref=o_buf.at[at_block(t), :], dst_ref=out.at[0, :, at_block(me)],
-            send_sem=out_send.at[t], recv_sem=out_recv.at[me], device_id={"ctx": t}, device_id_type=MESH,
+            send_sem=out_send, recv_sem=out_recv, device_id={"ctx": t}, device_id_type=MESH,
         )
 
     def out_own_copy():
@@ -290,16 +324,15 @@
         weigh(tile, q_full, k_full, s_buf, p_buf)
         mix(tile, p_buf, v_full, gains, o_buf)
 
-    own(1).wait()
-    remote(1, 1).wait_recv()
+    own_query().wait()
+    some_queries(0, TOK).wait_recv()
     attend(pair)
     out_own_copy().start()
     out_copy(partner(1)).start()
 
     def finish(n, carry):
         tile = lax.rem(pair + tiles - n, tiles)
-        remote(1, 2 * n).wait_recv()
-        remote(1, 2 * n + 1).wait_recv()
+        some_queries(n, ROWS).wait_recv()
         attend(tile)
         for h in range(2):
             out_copy(2 * tile + h).start()
@@ -307,19 +340,17 @@
 
     lax.fori_loop(1, tiles, finish, 0)
 
-    for a in range(5):
-        each_partner(lambda d, a=a: remote(a, d).wait_send())
-    each_partner(lambda d: out_copy(partner(d)).wait_send())
-
-    def out_arrived(d):
-        s = partner(d)
-        pltpu.make_async_remote_copy(
-            src_ref=o_buf.at[at_block(s), :], dst_ref=out.at[0, :, at_block(s)],
-            send_sem=out_send.at[s], recv_sem=out_recv.at[s], device_id={"ctx": s}, device_id_type=MESH,
-        ).wait_recv()
-
-    each_partner(out_arrived)
+    all_of(2).wait_send()
+    some_queries(0, LENGTH - TOK).wait_send()
+    sent = o_buf.at[pl.ds(0, LENGTH - TOK), :]
+    landed = out.at[0, :, pl.ds(0, LENGTH - TOK)]
+    back = pltpu.make_async_remote_copy(
+        src_ref=sent, dst_ref=landed, send_sem=out_send, recv_sem=out_recv,
+        device_id={"ctx": partner(1)}, device_id_type=MESH,
+    )
+    back.wait_send()
     out_own_copy().wait()
+    back.wait_recv()
 
 
 def local(queries, key_rows, value_rows, reflections, segment_ids, head_gains):
@@ -345,11 +376,13 @@
             pltpu.VMEM((ROWS, SPAN), F32),
             pltpu.VMEM((ROWS, SPAN), BF16),
             pltpu.VMEM((LENGTH, HD), BF16),
-            dma((5, BLOCKS)),
-            dma((5, BLOCKS)),
+            dma((4,)),
+            dma((4,)),
             dma((5,)),
-            dma((BLOCKS,)),
-            dma((BLOCKS,)),
+            dma,
+            dma((LENGTH // ROWS,)),
+            dma,
+            dma,
             dma,
             dma,
             dma,

time: 71.9 us -> 69.9 us (0.972)
  Pallas kernels: 71 us -> 69 us
    pallas_call x1, Pallas kernels: 71 us -> 69 us  [local(): pl.pallas_call(kernel, out_shape=pltpu.VMEM((1, TOK, HEADS * HD), BF16),...]
where the time goes in v4:
time: 69.9 us; the launch traced here: 69.8 us
  Pallas kernels  69 us (99%)
  local copies, waits for them, and re-layouts  0.8 us (1%)
    pallas_call x1, Pallas kernels, local(): pl.pallas_call(kernel, out_shape=pltpu.VMEM((1, TOK, HEADS * HD), BF16),...  69 us

profile of v4, /device:TPU:6, one launch (start us, length us, event | category | flops | bytes accessed | tf_op | source)
XLA Modules:
  0.0 69.8 jit_solution(4272098574921449373)
XLA Ops:
  0.0 69.0 %shard_map.64 = bf16[1,128,2048]{2,1,0:T(8,128)(2,1)S(1)} custom-call(bf16[1,128,2048]{2,1,0:T(8,128)(2,1)} %q_in.1, bf16[1,128,2048]{2,1,0:T(8,128)(2,1)} %k_in.1, bf16[1,128,2048]{2,1,0:T(8,128)(2,1)} %v_in.1, bf16[1,128,2048]{2,1,0:T(8,128)(2,1)} %r_in.1, s32[1,128]{1,0:T(1,128)} %segment_in.1, f32[1,128]{1,0:T(1,128)} %bitcast.1), custom_call_target="tpu_custom_call" | custom-call | tf_op jit(solution)/shard_map/pallas_call | solution.py:360
  69.0 0.8 %copy.8 = bf16[1,128,2048]{2,1,0:T(8,128)(2,1)} copy(bf16[1,128,2048]{2,1,0:T(8,128)(2,1)S(1)} %shard_map.64) | data formatting | bytes 1048576

commit v5 on v4

--- a/solution.py
+++ b/solution.py
@@ -18,6 +18,8 @@
 BLOCKS = LENGTH // TOK
 GROUP = 4
 EPSILON = 1e-06
+TURNS = (2, 6, 1, 7, 3, 5, 4)
+SENDS = (1,) + tuple(2 * n + e for n in TURNS for e in range(2))
 FAR = 2.0**100
 F32 = jnp.float32
 BF16 = jnp.bfloat16
@@ -241,13 +243,6 @@
             device_id=crossed, device_id_type=MESH,
         )
 
-    def each_partner(act):
-        def one(d, carry):
-            act(d)
-            return carry
-
-        lax.fori_loop(1, count, one, 0)
-
     def arrive(a):
         own(a).wait()
         all_of(a).wait_recv()
@@ -274,8 +269,10 @@
         pltpu.make_async_copy(gain_in, gains, gain_own).start()
 
     for a in (0, 3, 1, 2):
-        each_partner(lambda d, a=a: remote(a, d).start())
-    each_partner(lambda d: query(d).start())
+        for d in SENDS:
+            remote(a, d).start()
+    for d in SENDS:
+        query(d).start()
 
     prepare_bands(k_full, v_full)
     arrive(0)
@@ -330,7 +327,8 @@
     out_own_copy().start()
     out_copy(partner(1)).start()
 
-    def finish(n, carry):
+    def finish(turn, carry):
+        n = TURNS[turn - 1]
         tile = lax.rem(pair + tiles - n, tiles)
         some_queries(n, ROWS).wait_recv()
         attend(tile)
@@ -338,7 +336,8 @@
             out_copy(2 * tile + h).start()
         return carry
 
-    lax.fori_loop(1, tiles, finish, 0)
+    for turn in range(1, tiles):
+        finish(turn, 0)
 
     all_of(2).wait_send()
     some_queries(0, LENGTH - TOK).wait_send()

time: 69.9 us -> 69.6 us (level)
  no operation moved by 1% of the time
where the time goes in v5:
time: 69.6 us; the launch traced here: 69.5 us
  Pallas kernels  68.7 us (99%)
  local copies, waits for them, and re-layouts  0.8 us (1%)
    pallas_call x1, Pallas kernels, local(): pl.pallas_call(kernel, out_shape=pltpu.VMEM((1, TOK, HEADS * HD), BF16),...  68.7 us

profile of v5, /device:TPU:6, one launch (start us, length us, event | category | flops | bytes accessed | tf_op | source)
XLA Modules:
  0.0 69.5 jit_solution(1470424089267765686)
XLA Ops:
  0.0 68.7 %shard_map.64 = bf16[1,128,2048]{2,1,0:T(8,128)(2,1)S(1)} custom-call(bf16[1,128,2048]{2,1,0:T(8,128)(2,1)} %q_in.1, bf16[1,128,2048]{2,1,0:T(8,128)(2,1)} %k_in.1, bf16[1,128,2048]{2,1,0:T(8,128)(2,1)} %v_in.1, bf16[1,128,2048]{2,1,0:T(8,128)(2,1)} %r_in.1, s32[1,128]{1,0:T(1,128)} %segment_in.1, f32[1,128]{1,0:T(1,128)} %bitcast.1), custom_call_target="tpu_custom_call" | custom-call | tf_op jit(solution)/shard_map/pallas_call | solution.py:359
  68.7 0.8 %copy.8 = bf16[1,128,2048]{2,1,0:T(8,128)(2,1)} copy(bf16[1,128,2048]{2,1,0:T(8,128)(2,1)S(1)} %shard_map.64) | data formatting | bytes 1048576

commit v6 on v5

--- a/solution.py
+++ b/solution.py
@@ -253,7 +253,7 @@
     def _():
         pl.semaphore_signal(barrier, inc=1, device_id=crossed, device_id_type=MESH)
 
-    for d in range(1, count):
+    for d in SENDS[1:] + SENDS[:1]:
         pl.semaphore_signal(barrier, inc=1, device_id={"ctx": partner(d)}, device_id_type=MESH)
     for a in range(4):
         own(a).start()

time: 69.6 us -> 69.6 us (level)
  no operation moved by 1% of the time
where the time goes in v6:
time: 69.6 us; the launch traced here: 69.5 us
  Pallas kernels  68.7 us (99%)
  local copies, waits for them, and re-layouts  0.8 us (1%)
    pallas_call x1, Pallas kernels, local(): pl.pallas_call(kernel, out_shape=pltpu.VMEM((1, TOK, HEADS * HD), BF16),...  68.7 us

profile of v6, /device:TPU:6, one launch (start us, length us, event | category | flops | bytes accessed | tf_op | source)
XLA Modules:
  0.0 69.5 jit_solution(2551630147075579203)
XLA Ops:
  0.0 68.7 %shard_map.64 = bf16[1,128,2048]{2,1,0:T(8,128)(2,1)S(1)} custom-call(bf16[1,128,2048]{2,1,0:T(8,128)(2,1)} %q_in.1, bf16[1,128,2048]{2,1,0:T(8,128)(2,1)} %k_in.1, bf16[1,128,2048]{2,1,0:T(8,128)(2,1)} %v_in.1, bf16[1,128,2048]{2,1,0:T(8,128)(2,1)} %r_in.1, s32[1,128]{1,0:T(1,128)} %segment_in.1, f32[1,128]{1,0:T(1,128)} %bitcast.1), custom_call_target="tpu_custom_call" | custom-call | tf_op jit(solution)/shard_map/pallas_call | solution.py:359
  68.7 0.8 %copy.8 = bf16[1,128,2048]{2,1,0:T(8,128)(2,1)} copy(bf16[1,128,2048]{2,1,0:T(8,128)(2,1)S(1)} %shard_map.64) | data formatting | bytes 1048576
